TPU v7x, 1024 devices: a whole 4x4x32 slice. The times are simulated.
1024 devices in a mesh: dp: 64 (over z, core), dap: 16 (over y, x).
Axes of the slice: x: 4, y: 4, z: 32, core: 2. Of those that a mesh axis runs over, the one named last changes fastest.
Arguments:
- pair_rep: bfloat16 [8192, 128, 128], P(('dp', 'dap')), parts along dimension 0, may hold values from -6 to 6
- proj_weight: bfloat16 [2, 128, 512], replicated, may hold values from -0.5 to 0.5
- gate_weight: bfloat16 [2, 128, 128], replicated, may hold values from -0.5 to 0.5
- out_weight: bfloat16 [2, 128, 128], replicated, may hold values from -0.5 to 0.5
- norm_gain: float32 [2, 128], replicated, may hold values from 0.25 to 1.75
- mid_gain: float32 [2, 128], replicated, may hold values from 0.25 to 1.75
Outputs:
- pair_out: bfloat16 [8192, 128, 128], P(('dp', 'dap')), parts along dimension 0
There are 64 independent parts, one for each index of `dp`. A program takes and returns all parts, laid end to end along the dimension named above; an argument that names none is the same for every part. Nothing has to cross between parts.
All inputs are finite; a program needn't handle non-finite values.
Results may differ from a plain program's by a relative error of at most 0.017.
Values may be sent and summed in bfloat16 or wider, within the bound.
A program may use at most 32 MiB of HBM per device.

v0:
```python
import jax
import jax.numpy as jnp
from jax import lax
from jax.sharding import PartitionSpec as P


def normalize(values, gain):
    mean = jnp.mean(values, axis=-1, keepdims=True)
    centered = values - mean
    var = jnp.mean(centered * centered, axis=-1, keepdims=True)
    return centered * jax.lax.rsqrt(var + 1e-05) * gain


def project(normed, proj_w):
    hidden = proj_w.shape[1] // 4
    lead = normed.shape[:2]
    proj = jnp.dot(normed.reshape(-1, normed.shape[2]), proj_w, preferred_element_type=jnp.float32)
    proj = proj.reshape(lead[0], lead[1], 4 * hidden)
    left_proj = (jax.nn.sigmoid(proj[..., hidden : 2 * hidden]) * proj[..., :hidden]).astype(
        jnp.bfloat16
    )
    right_proj = (
        jax.nn.sigmoid(proj[..., 3 * hidden :]) * proj[..., 2 * hidden : 3 * hidden]
    ).astype(jnp.bfloat16)
    return (left_proj, right_proj)


def finish(pair_in, normed, mixed, gate_w, out_w, gain_mid):
    rows, size, chans = pair_in.shape
    hidden = out_w.shape[0]
    mid = normalize(mixed, gain_mid).astype(jnp.bfloat16)
    gate = jax.nn.sigmoid(
        jnp.dot(normed.reshape(-1, chans), gate_w, preferred_element_type=jnp.float32)
    )
    update = gate * jnp.dot(mid.reshape(-1, hidden), out_w, preferred_element_type=jnp.float32)
    return (pair_in.astype(jnp.float32) + update.reshape(rows, size, chans)).astype(jnp.bfloat16)


def per_device(pair_rep, proj_weight, gate_weight, out_weight, norm_gain, mid_gain):
    normed = normalize(pair_rep.astype(jnp.float32), norm_gain[0]).astype(jnp.bfloat16)
    left_proj, right_proj = project(normed, proj_weight[0])
    mixed = jnp.einsum(
        "ikc,jkc->ijc",
        left_proj,
        lax.all_gather(right_proj, "dap", axis=0, tiled=True),
        preferred_element_type=jnp.float32,
    )
    after_out = finish(pair_rep, normed, mixed, gate_weight[0], out_weight[0], mid_gain[0])
    normed_two = normalize(after_out.astype(jnp.float32), norm_gain[1]).astype(jnp.bfloat16)
    left_rows, right_rows = project(normed_two, proj_weight[1])
    left_cols, right_cols = (
        lax.all_to_all(left_rows, "dap", split_axis=1, concat_axis=0, tiled=True),
        lax.all_to_all(right_rows, "dap", split_axis=1, concat_axis=0, tiled=True),
    )
    mixed_two = jnp.einsum(
        "kic,kjc->ijc",
        left_cols,
        lax.all_gather(right_cols, "dap", axis=1, tiled=True),
        preferred_element_type=jnp.float32,
    )
    return finish(after_out, normed_two, mixed_two, gate_weight[1], out_weight[1], mid_gain[1])


def solution(mesh):
    return jax.shard_map(
        per_device,
        mesh=mesh,
        in_specs=(P(("dp", "dap"), None, None), P(), P(), P(), P(), P()),
        out_specs=P(("dp", "dap"), None, None),
        check_vma=False,
    )
```

profile of v0, /device:TPU:1, one launch (start us, length us, event | category | flops | bytes accessed | tf_op | source)
XLA Modules:
  0.0 241.0 jit_solution(7922952666404868519)
XLA Ops:
  6.5 1.1 convert_reduce_fusion.1
  7.7 1.3 fusion.13
  9.0 0.8 slice_bitcast_fusion.1
  9.8 1.3 fusion.15
  11.1 1.3 fusion.40
  12.4 1.0 fusion.26
  13.4 0.2 copy.24
  13.7 0.3 fusion.5
  14.0 95.3 %all-gather.3.cloned.1.call-done = bf16[128,128,128]{2,1,0:T(8,128)(2,1)} async-done(((bf16[8,128,128]{2,1,0:T(8,128)(2,1)}), bf16[128,128,128]{2,1,0:T(8,128)(2,1)}) %all-gather.3.cloned.1.call-update) | async-done | bytes 4194320 | tf_op jit(solution)/shard_map/all_gather | solution.py:45
  109.3 6.7 %copy.23 = bf16[128,128,128]{1,0,2:T(8,128)(2,1)} copy(bf16[128,128,128]{2,1,0:T(8,128)(2,1)} %all-gather.3.cloned.1.call-done) | data formatting | bytes 8388608 | tf_op jit(solution)/shard_map/all_gather | solution.py:45
  116.0 4.5 %fusion.53 = (f32[8,128]{1,0:T(8,128)S(1)}, f32[8,128,128]{1,0,2:T(8,128)S(1)}) fusion(bf16[128,128,128]{1,0,2:T(8,128)(2,1)} %copy.23, bf16[8,128,128]{1,0,2:T(8,128)(2,1)S(1)} %copy.24), kind=kOutput, calls=%fused_computation.88 | convolution fusion | flops 33684480 | bytes 4984832 | tf_op jit(solution)/shard_map/ikc,jkc->ijc/dot_general | solution.py:42
  120.5 0.2 multiply_reduce_fusion.1
  120.7 0.2 multiply_convert_fusion.1
  120.9 0.3 convolution_multiply_fusion.1
  121.2 0.2 convert_reduce_fusion
  121.4 0.4 fusion.10
  121.8 0.3 fusion.12
  122.2 0.4 fusion.38
  122.6 0.3 fusion.18
  122.9 0.2 copy.25
  123.1 12.3 %all_to_all.36 = bf16[8,128,128]{2,0,1:T(8,128)(2,1)S(1)} all-to-all(bf16[8,128,128]{2,0,1:T(8,128)(2,1)S(1)} %copy.25), channel_id=1, replica_groups=mesh['dp'=64,'dap'=16] {'dap'}, dimensions={1} | all-to-all | bytes 524288 | tf_op jit(solution)/shard_map/all_to_all | solution.py:53
  135.5 0.9 copy.28
  136.4 0.9 copy.29
  137.3 3.5 %all-to-all-start.1 = ((bf16[8,128,128]{2,0,1:T(8,128)(2,1)}), bf16[8,128,128]{2,0,1:T(8,128)(2,1)S(1)}, u32[]{:S(2)}, u32[]{:S(2)}) async-start(bf16[8,128,128]{2,0,1:T(8,128)(2,1)} %copy.29), calls=%async_computation.1 | async-start | bytes 524288 | tf_op jit(solution)/shard_map/all_to_all | solution.py:52
  140.8 0.3 fusion.2
  141.1 7.2 %all-to-all-done.1 = bf16[8,128,128]{2,0,1:T(8,128)(2,1)S(1)} async-done(((bf16[8,128,128]{2,0,1:T(8,128)(2,1)}), bf16[8,128,128]{2,0,1:T(8,128)(2,1)S(1)}, u32[]{:S(2)}, u32[]{:S(2)}) %all-to-all-start.1) | async-done | bytes 262176 | tf_op jit(solution)/shard_map/all_to_all | solution.py:52
  148.4 0.2 copy.32
  148.6 79.7 %all-gather.5.cloned.1.call-done = bf16[128,128,128]{0,1,2:T(8,128)(2,1)} async-done(((bf16[128,8,128]{0,1,2:T(8,128)(2,1)}), bf16[128,128,128]{0,1,2:T(8,128)(2,1)}) %all-gather.5.cloned.1.call-update) | async-done | bytes 4194320 | tf_op jit(solution)/shard_map/all_gather | solution.py:58
  228.3 4.4 %fusion.54 = (f32[8,128]{1,0:T(8,128)S(1)}, f32[8,128,128]{1,0,2:T(8,128)S(1)}) fusion(bf16[128,128,128]{0,1,2:T(8,128)(2,1)} %all-gather.5.cloned.1.call-done, bf16[128,8,128]{0,1,2:T(8,128)(2,1)S(1)} %copy.32), kind=kOutput, calls=%fused_computation.89 | convolution fusion | flops 33684480 | bytes 4984832 | tf_op jit(solution)/shard_map/kic,kjc->ijc/dot_general | solution.py:55
  232.9 0.2 multiply_convert_fusion
  233.1 0.3 convolution_multiply_fusion
  233.4 0.8 fusion.17
  (26 shorter events, 0.4 us)
Async XLA Ops:
  6.5 7.1 %copy-start.3 = (f32[2,128]{1,0:T(2,128)S(1)}, f32[2,128]{1,0:T(2,128)}, u32[]{:S(2)}) copy-start(f32[2,128]{1,0:T(2,128)} %param.11) | copy-start | bytes 3076
  6.5 7.1 %copy-start.4 = (bf16[2,128,128]{2,1,0:T(8,128)(2,1)S(1)}, bf16[2,128,128]{2,1,0:T(8,128)(2,1)}, u32[]{:S(2)}) copy-start(bf16[2,128,128]{2,1,0:T(8,128)(2,1)} %param.8) | copy-start | bytes 196612
  6.5 102.8 %all-gather.3.cloned.1.call-start = ((), (), s32[]{:S(2)}) async-start(), calls=%async_computation.2 | async-start | bytes 4456448 | tf_op jit(solution)/shard_map/all_gather | solution.py:45
  13.4 214.9 %all-gather.5.cloned.1.call-start = ((), (), s32[]{:S(2)}) async-start(), calls=%async_computation.3 | async-start | bytes 4456448 | tf_op jit(solution)/shard_map/all_gather | solution.py:58
  116.0 4.9 %copy-start.2 = (bf16[2,128,128]{2,1,0:T(8,128)(2,1)S(1)}, bf16[2,128,128]{2,1,0:T(8,128)(2,1)}, u32[]{:S(2)}) copy-start(bf16[2,128,128]{2,1,0:T(8,128)(2,1)} %param.9) | copy-start | bytes 196612
  116.0 5.2 %copy-start = (bf16[8,128,128]{2,1,0:T(8,128)(2,1)S(1)}, bf16[8,128,128]{2,1,0:T(8,128)(2,1)}, u32[]{:S(2)}) copy-start(bf16[8,128,128]{2,1,0:T(8,128)(2,1)} %param.6) | copy-start | bytes 786436
  116.0 6.1 %copy-start.1 = (bf16[2,128,512]{2,1,0:T(8,128)(2,1)S(1)}, bf16[2,128,512]{2,1,0:T(8,128)(2,1)}, u32[]{:S(2)}) copy-start(bf16[2,128,512]{2,1,0:T(8,128)(2,1)} %param.7) | copy-start | bytes 786436
  137.3 11.0 %all-to-all-start.1 = ((bf16[8,128,128]{2,0,1:T(8,128)(2,1)}), bf16[8,128,128]{2,0,1:T(8,128)(2,1)S(1)}, u32[]{:S(2)}, u32[]{:S(2)}) async-start(bf16[8,128,128]{2,0,1:T(8,128)(2,1)} %copy.29), calls=%async_computation.1 | async-start | bytes 524288 | tf_op jit(solution)/shard_map/all_to_all | solution.py:52
Sparse Core Ops, SparseCore 0:
  13.5 95.7 all-gather.2
  136.5 91.7 all-gather.4
where the time goes:
time: 242 us; the launch traced here: 241 us
  waiting for transfers between devices  182 us (75%)
  between operations  13.6 us (6%)
  blocking collectives  12.3 us (5%)
  matrix products  11.7 us (5%)
  local copies, waits for them, and re-layouts  10 us (4%)
  other arithmetic  7.5 us (3%)
  starting transfers between devices  3.57 us (1%)
    all_gather x1, waiting for transfers between devices, per_device(): lax.all_gather(right_proj, 'dap', axis=0, tiled=True)  95.3 us
    all_gather x1, waiting for transfers between devices, per_device(): lax.all_gather(right_cols, 'dap', axis=1, tiled=True)  79.7 us
    all_to_all x1, blocking collectives, per_device(): lax.all_to_all(right_rows, 'dap', split_axis=1, concat_axis=0, tiled=True)  12.3 us
    all_to_all x1, waiting for transfers between devices, per_device(): lax.all_to_all(left_rows, 'dap', split_axis=1, concat_axis=0, tiled=True)  7.21 us
    all_gather x1, local copies, waits for them, and re-layouts, per_device(): lax.all_gather(right_proj, 'dap', axis=0, tiled=True)  6.72 us
  transfers between devices with their start and end apart: 3, of which 3 were waited for; matrix products, arithmetic and copies ran while one was open for 1% of the time, Pallas kernels for 0%

commit v1 on v0

v1 whole, which is shorter than its diff:
```python
import jax
import jax.numpy as jnp
from jax import lax
from jax.experimental import pallas as pl
from jax.experimental.pallas import tpu as pltpu
from jax.sharding import PartitionSpec as P

MESH = pl.DeviceIdType.MESH
BF16 = jnp.bfloat16
F32 = jnp.float32
SIDE = 4
GROUP = SIDE * SIDE
RES = 128
CHANS = 128
ROWS = RES // GROUP
OWN = CHANS // GROUP


def far_first(offset):
    return -sum(min(step, SIDE - step) for step in offset)


OFFSETS = sorted(
    [(dy, dx) for dy in range(SIDE) for dx in range(SIDE) if (dy, dx) != (0, 0)], key=far_first
)


def contract(lhs, rhs, lhs_dim, rhs_dim):
    return lax.dot_general(
        lhs, rhs, (((lhs_dim,), (rhs_dim,)), ((), ())), preferred_element_type=F32
    )


def kernel(
    pair, proj_w, gate_w, out_w, norm_gain, mid_gain, result,
    proj_t, gate_t, out_t, gains, chan_pair, chan_normed, chan_gate, row_gate, row_pair,
    send_proj, recv_proj, send_mix, recv_mix, wide_proj, wide_mix, stats, send_sem, recv_sem,
):
    crop = lax.axis_index("dp")
    me = lax.axis_index("dap")
    y, x = me // SIDE, lax.rem(me, SIDE)

    def towards(offset):
        return lax.rem(y + offset[0], SIDE) * SIDE + lax.rem(x + offset[1], SIDE)

    def back(offset):
        return towards((SIDE - offset[0], SIDE - offset[1]))

    barrier = pltpu.get_barrier_semaphore()
    for offset in OFFSETS:
        pl.semaphore_signal(
            barrier, inc=1, device_id=(crop, towards(offset)), device_id_type=MESH
        )

    def exchange(phase, source, target):
        copies = []
        for n, offset in enumerate(OFFSETS):
            there = towards(offset)
            copy = pltpu.make_async_remote_copy(
                src_ref=source.at[there],
                dst_ref=target.at[me],
                send_sem=send_sem.at[phase, n],
                recv_sem=recv_sem.at[phase, n],
                device_id=(crop, there),
                device_id_type=MESH,
            )
            copy.start()
            copies.append(copy)
        return copies

    def column(row):
        return jnp.broadcast_to(row, (CHANS, CHANS)).T

    def turn_projection(block):
        for part in range(4):
            piece = proj_w[block, :, part * CHANS : (part + 1) * CHANS].astype(F32)
            proj_t[block, part] = (piece.T * 0.5).astype(BF16)

    def project(block, step, values):
        mean = jnp.mean(values, axis=0, keepdims=True)
        centered = values - mean
        var = jnp.mean(centered * centered, axis=0, keepdims=True)
        gain = gains[block]
        normed = centered * lax.rsqrt(var + 1e-05) * jnp.concatenate([gain, gain], axis=1)
        normed = normed.astype(BF16)
        chan_normed[:, step * 256 : (step + 1) * 256] = normed
        sides = []
        for side in range(2):
            half_value = contract(proj_t[block, 2 * side], normed, 1, 0)
            half_gate = contract(proj_t[block, 2 * side + 1], normed, 1, 0)
            sides.append(half_value * jnp.tanh(half_gate) + half_value)
        for h in range(2):
            parts = [s[:, h * RES : (h + 1) * RES].reshape(GROUP, OWN, RES) for s in sides]
            send_proj[block, :, 2 * step + h] = jnp.concatenate(parts, axis=1).astype(BF16)

    def widen(block, source, origin):
        wide_proj[pl.ds(pl.multiple_of(origin * RES, RES), RES), :] = (
            source[...].astype(F32).reshape(RES, RES)
        )

    def mix(block, copies):
        widen(block, send_proj.at[block, me], me)
        for n, offset in enumerate(OFFSETS):
            copies[n].wait_recv()
            origin = back(offset)
            widen(block, recv_proj.at[block, origin], origin)
        over = 1 if block == 0 else 0
        for pair_of in range(OWN // 2):
            mixed = []
            for c in (2 * pair_of, 2 * pair_of + 1):
                left = wide_proj[pl.ds(c, RES, stride=2 * OWN), :].astype(BF16)
                right = wide_proj[pl.ds(OWN + c, RES, stride=2 * OWN), :].astype(BF16)
                mixed.append(contract(left, right, over, over).reshape(GROUP, ROWS, RES))
            send_mix[block, :, pair_of] = jnp.concatenate(mixed, axis=1).astype(BF16)

    def gather_mixed(block, copies):
        def take(source, origin):
            values = source[...].astype(F32).reshape(OWN * ROWS, RES)
            wide_mix[pl.ds(pl.multiple_of(origin * OWN * ROWS, OWN * ROWS), OWN * ROWS), :] = values
            return jnp.sum(values.reshape(OWN, ROWS, RES), axis=0)

        total = take(send_mix.at[block, me], me)
        for n, offset in enumerate(OFFSETS):
            copies[n].wait_recv()
            origin = back(offset)
            total = total + take(recv_mix.at[block, origin], origin)
        mean = total * (1.0 / CHANS)
        spread = jnp.zeros_like(mean)
        for part in range(GROUP):
            size = OWN * ROWS
            values = wide_mix[part * size : (part + 1) * size, :].reshape(OWN, ROWS, RES) - mean
            spread = spread + jnp.sum(values * values, axis=0)
        stats[0] = mean
        stats[1] = lax.rsqrt(spread * (1.0 / CHANS) + 1e-05)

    def mid_row(block, i):
        values = wide_mix[pl.ds(i, CHANS, stride=ROWS), :]
        mean, scale = stats[0, i : i + 1, :], stats[1, i : i + 1, :]
        return ((values - mean) * scale * gains[2 + block]).astype(BF16)

    gains[0] = column(norm_gain[0:1, :])
    turn_projection(0)
    for step in range(ROWS // 2):
        turned = [pair[2 * step + h].astype(F32).T for h in range(2)]
        values = jnp.concatenate(turned, axis=1)
        chan_pair[:, step * 256 : (step + 1) * 256] = values
        project(0, step, values)

    pl.semaphore_wait(barrier, len(OFFSETS))
    copies_a = exchange(0, send_proj.at[0], recv_proj.at[0])

    gains[1] = column(norm_gain[1:2, :])
    gains[2] = column(mid_gain[0:1, :])
    gains[3] = column(mid_gain[1:2, :])
    turn_projection(1)
    gate_t[...] = (gate_w[0].astype(F32).T * 0.5).astype(BF16)
    out_t[...] = out_w[0].astype(F32).T.astype(BF16)
    for step in range(ROWS // 2):
        at = slice(step * 256, (step + 1) * 256)
        chan_gate[:, at] = 0.5 * jnp.tanh(contract(gate_t[...], chan_normed[:, at], 1, 0)) + 0.5

    mix(0, copies_a)
    copies_b = exchange(1, send_mix.at[0], recv_mix.at[0])
    gather_mixed(0, copies_b)
    for step in range(ROWS // 2):
        at = slice(step * 256, (step + 1) * 256)
        mid = jnp.concatenate([mid_row(0, 2 * step), mid_row(0, 2 * step + 1)], axis=1)
        update = chan_gate[:, at] * contract(out_t[...], mid, 1, 0)
        values = (chan_pair[:, at] + update).astype(BF16).astype(F32)
        chan_pair[:, at] = values
        project(1, step, values)

    copies_c = exchange(2, send_proj.at[1], recv_proj.at[1])
    half_gate_w = (gate_w[1].astype(F32) * 0.5).astype(BF16)
    for i in range(ROWS):
        at = slice(i * RES, (i + 1) * RES)
        row_gate[i] = 0.5 * jnp.tanh(contract(chan_normed[:, at], half_gate_w, 0, 0)) + 0.5
        row_pair[i] = chan_pair[:, at].T
    mix(1, copies_c)
    copies_d = exchange(3, send_mix.at[1], recv_mix.at[1])
    gather_mixed(1, copies_d)
    for i in range(ROWS):
        update = row_gate[i] * contract(mid_row(1, i), out_w[1], 0, 0)
        result[i] = (row_pair[i] + update).astype(BF16)

    for copies in (copies_a, copies_b, copies_c, copies_d):
        for copy in copies:
            copy.wait_send()


def per_device(pair_rep, proj_weight, gate_weight, out_weight, norm_gain, mid_gain):
    vmem = pl.BlockSpec(memory_space=pltpu.VMEM)
    return pl.pallas_call(
        kernel,
        out_shape=jax.ShapeDtypeStruct((ROWS, RES, CHANS), BF16),
        in_specs=[vmem] * 6,
        out_specs=vmem,
        scratch_shapes=[
            pltpu.VMEM((2, 4, CHANS, CHANS), BF16),
            pltpu.VMEM((CHANS, CHANS), BF16),
            pltpu.VMEM((CHANS, CHANS), BF16),
            pltpu.VMEM((4, CHANS, CHANS), F32),
            pltpu.VMEM((CHANS, ROWS * RES), F32),
            pltpu.VMEM((CHANS, ROWS * RES), BF16),
            pltpu.VMEM((CHANS, ROWS * RES), F32),
            pltpu.VMEM((ROWS, RES, CHANS), F32),
            pltpu.VMEM((ROWS, RES, CHANS), F32),
            pltpu.VMEM((2, GROUP, ROWS, 2 * OWN, RES), BF16),
            pltpu.VMEM((2, GROUP, ROWS, 2 * OWN, RES), BF16),
            pltpu.VMEM((2, GROUP, OWN // 2, 2 * ROWS, RES), BF16),
            pltpu.VMEM((2, GROUP, OWN // 2, 2 * ROWS, RES), BF16),
            pltpu.VMEM((RES * 2 * OWN, RES), F32),
            pltpu.VMEM((CHANS * ROWS, RES), F32),
            pltpu.VMEM((2, ROWS, RES), F32),
            pltpu.SemaphoreType.DMA((4, len(OFFSETS))),
            pltpu.SemaphoreType.DMA((4, len(OFFSETS))),
        ],
        compiler_params=pltpu.CompilerParams(
            collective_id=0, has_side_effects=True, vmem_limit_bytes=32 * 1024 * 1024
        ),
        name="triangles",
    )(pair_rep, proj_weight, gate_weight, out_weight, norm_gain, mid_gain)


def solution(mesh):
    return jax.shard_map(
        per_device,
        mesh=mesh,
        in_specs=(P(("dp", "dap"), None, None), P(), P(), P(), P(), P()),
        out_specs=P(("dp", "dap"), None, None),
        check_vma=False,
    )
```

time: 242 us -> 51.5 us (0.21)
  the two profiles are of different devices: /device:TPU:1 before, /device:TPU:2 now
where the time goes in v1:
time: 51.5 us; the launch traced here: 51.2 us
  Pallas kernels  45.5 us (88%)
  local copies, waits for them, and re-layouts  5.64 us (11%)
    pallas_call x1, Pallas kernels, per_device(): pl.pallas_call(kernel, out_shape=jax.ShapeDtypeStruct((ROWS, RES, CHANS),...  45.5 us
    unnamed x13, local copies, waits for them, and re-layouts  5.64 us

profile of v1, /device:TPU:2, one launch (start us, length us, event | category | flops | bytes accessed | tf_op | source)
XLA Modules:
  0.0 51.2 jit_solution(10867062645429098089)
XLA Ops:
  0.0 0.0 copy-start
  0.0 0.9 %copy-done = bf16[8,128,128]{2,1,0:T(8,128)(2,1)S(1)} copy-done((bf16[8,128,128]{2,1,0:T(8,128)(2,1)S(1)}, bf16[8,128,128]{2,1,0:T(8,128)(2,1)}, u32[]{:S(2)}) %copy-start) | copy-done | bytes 262168
  1.0 0.0 copy-start.1
  1.0 0.9 %copy-done.1 = bf16[2,128,512]{2,1,0:T(8,128)(2,1)S(1)} copy-done((bf16[2,128,512]{2,1,0:T(8,128)(2,1)S(1)}, bf16[2,128,512]{2,1,0:T(8,128)(2,1)}, u32[]{:S(2)}) %copy-start.1) | copy-done | bytes 262168
  1.9 0.0 copy-start.2
  1.9 0.8 %copy-done.2 = bf16[2,128,128]{2,1,0:T(8,128)(2,1)S(1)} copy-done((bf16[2,128,128]{2,1,0:T(8,128)(2,1)S(1)}, bf16[2,128,128]{2,1,0:T(8,128)(2,1)}, u32[]{:S(2)}) %copy-start.2) | copy-done | bytes 65560
  2.7 0.0 copy-start.3
  2.7 0.8 %copy-done.3 = bf16[2,128,128]{2,1,0:T(8,128)(2,1)S(1)} copy-done((bf16[2,128,128]{2,1,0:T(8,128)(2,1)S(1)}, bf16[2,128,128]{2,1,0:T(8,128)(2,1)}, u32[]{:S(2)}) %copy-start.3) | copy-done | bytes 65560
  3.6 0.0 copy-start.4
  3.6 0.7 %copy-done.4 = f32[2,128]{1,0:T(2,128)S(1)} copy-done((f32[2,128]{1,0:T(2,128)S(1)}, f32[2,128]{1,0:T(2,128)}, u32[]{:S(2)}) %copy-start.4) | copy-done | bytes 1048
  4.3 0.0 copy-start.5
  4.3 0.7 %copy-done.5 = f32[2,128]{1,0:T(2,128)S(1)} copy-done((f32[2,128]{1,0:T(2,128)S(1)}, f32[2,128]{1,0:T(2,128)}, u32[]{:S(2)}) %copy-start.5) | copy-done | bytes 1048
  4.9 45.5 %triangles.1 = bf16[8,128,128]{2,1,0:T(8,128)(2,1)S(1)} custom-call(bf16[8,128,128]{2,1,0:T(8,128)(2,1)S(1)} %copy-done, bf16[2,128,512]{2,1,0:T(8,128)(2,1)S(1)} %copy-done.1, bf16[2,128,128]{2,1,0:T(8,128)(2,1)S(1)} %copy-done.2, bf16[2,128,128]{2,1,0:T(8,128)(2,1)S(1)} %copy-done.3, f32[2,128]{1,0:T(2,128)S(1)} %copy-done.4, f32[2,128]{1,0:T(2,128)S(1)} %copy-done.5), custom_call_target="tpu_custom_call" | custom-call | tf_op jit(solution)/shard_map/triangles/pallas_call | solution.py:193
  50.5 0.7 %copy.8 = bf16[8,128,128]{2,1,0:T(8,128)(2,1)} copy(bf16[8,128,128]{2,1,0:T(8,128)(2,1)S(1)} %triangles.1) | data formatting | bytes 524288
Async XLA Ops:
  0.0 0.9 %copy-start = (bf16[8,128,128]{2,1,0:T(8,128)(2,1)S(1)}, bf16[8,128,128]{2,1,0:T(8,128)(2,1)}, u32[]{:S(2)}) copy-start(bf16[8,128,128]{2,1,0:T(8,128)(2,1)} %pair.1) | copy-start | bytes 786436
  1.0 0.9 %copy-start.1 = (bf16[2,128,512]{2,1,0:T(8,128)(2,1)S(1)}, bf16[2,128,512]{2,1,0:T(8,128)(2,1)}, u32[]{:S(2)}) copy-start(bf16[2,128,512]{2,1,0:T(8,128)(2,1)} %proj_w.1) | copy-start | bytes 786436
  1.9 0.8 %copy-start.2 = (bf16[2,128,128]{2,1,0:T(8,128)(2,1)S(1)}, bf16[2,128,128]{2,1,0:T(8,128)(2,1)}, u32[]{:S(2)}) copy-start(bf16[2,128,128]{2,1,0:T(8,128)(2,1)} %gate_w.1) | copy-start | bytes 196612
  2.7 0.8 %copy-start.3 = (bf16[2,128,128]{2,1,0:T(8,128)(2,1)S(1)}, bf16[2,128,128]{2,1,0:T(8,128)(2,1)}, u32[]{:S(2)}) copy-start(bf16[2,128,128]{2,1,0:T(8,128)(2,1)} %out_w.1) | copy-start | bytes 196612
  3.6 0.7 %copy-start.4 = (f32[2,128]{1,0:T(2,128)S(1)}, f32[2,128]{1,0:T(2,128)}, u32[]{:S(2)}) copy-start(f32[2,128]{1,0:T(2,128)} %norm_gain.1) | copy-start | bytes 3076
  4.3 0.7 %copy-start.5 = (f32[2,128]{1,0:T(2,128)S(1)}, f32[2,128]{1,0:T(2,128)}, u32[]{:S(2)}) copy-start(f32[2,128]{1,0:T(2,128)} %mid_gain.1) | copy-start | bytes 3076

commit v2 on v1

--- a/solution.py
+++ b/solution.py
@@ -32,8 +32,8 @@
 
 
 def kernel(
-    pair, proj_w, gate_w, out_w, norm_gain, mid_gain, result,
-    proj_t, gate_t, out_t, gains, chan_pair, chan_normed, chan_gate, row_gate, row_pair,
+    pair_hbm, proj_hbm, gate_hbm, out_hbm, norm_hbm, mid_hbm, result,
+    pair, proj_w, gate_w, out_w, norm_gain, mid_gain, load_sem, proj_t, gate_t, out_t, gains, chan_pair, chan_normed, chan_gate, row_gate, row_pair,
     send_proj, recv_proj, send_mix, recv_mix, wide_proj, wide_mix, stats, send_sem, recv_sem,
 ):
     crop = lax.axis_index("dp")
@@ -45,6 +45,14 @@
 
     def back(offset):
         return towards((SIDE - offset[0], SIDE - offset[1]))
+
+    places = (
+        (pair_hbm, pair), (proj_hbm, proj_w), (norm_hbm, norm_gain),
+        (mid_hbm, mid_gain), (gate_hbm, gate_w), (out_hbm, out_w),
+    )
+    loads = [pltpu.make_async_copy(*place, load_sem.at[n]) for n, place in enumerate(places)]
+    for load in loads:
+        load.start()
 
     barrier = pltpu.get_barrier_semaphore()
     for offset in OFFSETS:
@@ -138,6 +146,8 @@
         mean, scale = stats[0, i : i + 1, :], stats[1, i : i + 1, :]
         return ((values - mean) * scale * gains[2 + block]).astype(BF16)
 
+    for load in (loads[2], loads[1], loads[0]):
+        load.wait()
     gains[0] = column(norm_gain[0:1, :])
     turn_projection(0)
     for step in range(ROWS // 2):
@@ -149,6 +159,8 @@
     pl.semaphore_wait(barrier, len(OFFSETS))
     copies_a = exchange(0, send_proj.at[0], recv_proj.at[0])
 
+    for load in loads[3:]:
+        load.wait()
     gains[1] = column(norm_gain[1:2, :])
     gains[2] = column(mid_gain[0:1, :])
     gains[3] = column(mid_gain[1:2, :])
@@ -193,9 +205,16 @@
     return pl.pallas_call(
         kernel,
         out_shape=jax.ShapeDtypeStruct((ROWS, RES, CHANS), BF16),
-        in_specs=[vmem] * 6,
+        in_specs=[pl.BlockSpec(memory_space=pltpu.HBM)] * 6,
         out_specs=vmem,
         scratch_shapes=[
+            pltpu.VMEM((ROWS, RES, CHANS), BF16),
+            pltpu.VMEM((2, CHANS, 4 * CHANS), BF16),
+            pltpu.VMEM((2, CHANS, CHANS), BF16),
+            pltpu.VMEM((2, CHANS, CHANS), BF16),
+            pltpu.VMEM((2, CHANS), F32),
+            pltpu.VMEM((2, CHANS), F32),
+            pltpu.SemaphoreType.DMA((6,)),
             pltpu.VMEM((2, 4, CHANS, CHANS), BF16),
             pltpu.VMEM((CHANS, CHANS), BF16),
             pltpu.VMEM((CHANS, CHANS), BF16),
@@ -216,7 +235,7 @@
             pltpu.SemaphoreType.DMA((4, len(OFFSETS))),
         ],
         compiler_params=pltpu.CompilerParams(
-            collective_id=0, has_side_effects=True, vmem_limit_bytes=32 * 1024 * 1024
+            collective_id=0, has_side_effects=True, vmem_limit_bytes=63 * 1024 * 1024
         ),
         name="triangles",
     )(pair_rep, proj_weight, gate_weight, out_weight, norm_gain, mid_gain)

time: 51.5 us -> 48.1 us (0.934)
  local copies, waits for them, and re-layouts: 5.64 us -> 1.67 us
  Pallas kernels: 45.5 us -> 46.2 us
    unnamed x13 -> x1, local copies, waits for them, and re-layouts: 5.64 us -> 1.67 us
    pallas_call x1, Pallas kernels: 45.5 us -> 46.2 us  [per_device(): pl.pallas_call(kernel, out_shape=jax.ShapeDtypeStruct((ROWS, RES, CHANS),...]
where the time goes in v2:
time: 48.1 us; the launch traced here: 47.9 us
  Pallas kernels  46.2 us (96%)
  local copies, waits for them, and re-layouts  1.67 us (3%)
    pallas_call x1, Pallas kernels, per_device(): pl.pallas_call(kernel, out_shape=jax.ShapeDtypeStruct((ROWS, RES, CHANS),...  46.2 us
    unnamed x1, local copies, waits for them, and re-layouts  1.67 us

profile of v2, /device:TPU:2, one launch (start us, length us, event | category | flops | bytes accessed | tf_op | source)
XLA Modules:
  0.0 47.9 jit_solution(14593143430806180328)
XLA Ops:
  0.0 46.2 %triangles.1 = bf16[8,128,128]{2,1,0:T(8,128)(2,1)} custom-call(bf16[8,128,128]{2,1,0:T(8,128)(2,1)} %pair_hbm.1, bf16[2,128,512]{2,1,0:T(8,128)(2,1)} %proj_hbm.1, bf16[2,128,128]{2,1,0:T(8,128)(2,1)} %gate_hbm.1, bf16[2,128,128]{2,1,0:T(8,128)(2,1)} %out_hbm.1, f32[2,128]{1,0:T(2,128)} %norm_hbm.1, f32[2,128]{1,0:T(2,128)} %mid_hbm.1), custom_call_target="tpu_custom_call" | custom-call | tf_op jit(solution)/shard_map/triangles/pallas_call | solution.py:205
  46.2 1.7 %copy.8 = bf16[8,128,128]{2,1,0:T(8,128)(2,1)} copy(bf16[8,128,128]{2,1,0:T(8,128)(2,1)} %triangles.1) | data formatting | bytes 524288

commit v3 on v2

--- a/solution.py
+++ b/solution.py
@@ -43,9 +43,6 @@
     def towards(offset):
         return lax.rem(y + offset[0], SIDE) * SIDE + lax.rem(x + offset[1], SIDE)
 
-    def back(offset):
-        return towards((SIDE - offset[0], SIDE - offset[1]))
-
     places = (
         (pair_hbm, pair), (proj_hbm, proj_w), (norm_hbm, norm_gain),
         (mid_hbm, mid_gain), (gate_hbm, gate_w), (out_hbm, out_w),
@@ -61,20 +58,35 @@
         )
 
     def exchange(phase, source, target):
-        copies = []
-        for n, offset in enumerate(OFFSETS):
+        for offset in OFFSETS:
             there = towards(offset)
             copy = pltpu.make_async_remote_copy(
                 src_ref=source.at[there],
                 dst_ref=target.at[me],
-                send_sem=send_sem.at[phase, n],
-                recv_sem=recv_sem.at[phase, n],
+                send_sem=send_sem.at[phase],
+                recv_sem=recv_sem.at[phase],
                 device_id=(crop, there),
                 device_id_type=MESH,
             )
             copy.start()
-            copies.append(copy)
-        return copies
+        target[me] = source[me]
+
+    def send_half(half, source, target, sem):
+        rows = pl.ds(half * (ROWS // 2), ROWS // 2)
+        for offset in OFFSETS:
+            there = towards(offset)
+            pltpu.make_async_remote_copy(
+                src_ref=source.at[there, rows],
+                dst_ref=target.at[me, rows],
+                send_sem=send_sem.at[sem],
+                recv_sem=recv_sem.at[sem],
+                device_id=(crop, there),
+                device_id_type=MESH,
+            ).start()
+
+    def all_of(sem, buffer):
+        blocks = buffer.at[pl.ds(0, len(OFFSETS))]
+        pltpu.make_async_copy(blocks, blocks, sem).wait()
 
     def column(row):
         return jnp.broadcast_to(row, (CHANS, CHANS)).T
@@ -101,17 +113,12 @@
             parts = [s[:, h * RES : (h + 1) * RES].reshape(GROUP, OWN, RES) for s in sides]
             send_proj[block, :, 2 * step + h] = jnp.concatenate(parts, axis=1).astype(BF16)
 
-    def widen(block, source, origin):
-        wide_proj[pl.ds(pl.multiple_of(origin * RES, RES), RES), :] = (
-            source[...].astype(F32).reshape(RES, RES)
-        )
-
-    def mix(block, copies):
-        widen(block, send_proj.at[block, me], me)
-        for n, offset in enumerate(OFFSETS):
-            copies[n].wait_recv()
-            origin = back(offset)
-            widen(block, recv_proj.at[block, origin], origin)
+    def mix(block):
+        all_of(recv_sem.at[2 * block], recv_proj.at[block])
+        for origin in range(GROUP):
+            wide_proj[origin * RES : (origin + 1) * RES, :] = (
+                recv_proj[block, origin].astype(F32).reshape(RES, RES)
+            )
         over = 1 if block == 0 else 0
         for pair_of in range(OWN // 2):
             mixed = []
@@ -121,22 +128,18 @@
                 mixed.append(contract(left, right, over, over).reshape(GROUP, ROWS, RES))
             send_mix[block, :, pair_of] = jnp.concatenate(mixed, axis=1).astype(BF16)
 
-    def gather_mixed(block, copies):
-        def take(source, origin):
-            values = source[...].astype(F32).reshape(OWN * ROWS, RES)
-            wide_mix[pl.ds(pl.multiple_of(origin * OWN * ROWS, OWN * ROWS), OWN * ROWS), :] = values
-            return jnp.sum(values.reshape(OWN, ROWS, RES), axis=0)
-
-        total = take(send_mix.at[block, me], me)
-        for n, offset in enumerate(OFFSETS):
-            copies[n].wait_recv()
-            origin = back(offset)
-            total = total + take(recv_mix.at[block, origin], origin)
+    def gather_mixed(block):
+        all_of(recv_sem.at[2 * block + 1], recv_mix.at[block])
+        size = OWN * ROWS
+        total = jnp.zeros((ROWS, RES), F32)
+        for origin in range(GROUP):
+            values = recv_mix[block, origin].astype(F32).reshape(size, RES)
+            wide_mix[origin * size : (origin + 1) * size, :] = values
+            total = total + jnp.sum(values.reshape(OWN, ROWS, RES), axis=0)
         mean = total * (1.0 / CHANS)
         spread = jnp.zeros_like(mean)
-        for part in range(GROUP):
-            size = OWN * ROWS
-            values = wide_mix[part * size : (part + 1) * size, :].reshape(OWN, ROWS, RES) - mean
+        for origin in range(GROUP):
+            values = wide_mix[origin * size : (origin + 1) * size, :].reshape(OWN, ROWS, RES) - mean
             spread = spread + jnp.sum(values * values, axis=0)
         stats[0] = mean
         stats[1] = lax.rsqrt(spread * (1.0 / CHANS) + 1e-05)
@@ -157,7 +160,7 @@
         project(0, step, values)
 
     pl.semaphore_wait(barrier, len(OFFSETS))
-    copies_a = exchange(0, send_proj.at[0], recv_proj.at[0])
+    exchange(0, send_proj.at[0], recv_proj.at[0])
 
     for load in loads[3:]:
         load.wait()
@@ -171,9 +174,9 @@
         at = slice(step * 256, (step + 1) * 256)
         chan_gate[:, at] = 0.5 * jnp.tanh(contract(gate_t[...], chan_normed[:, at], 1, 0)) + 0.5
 
-    mix(0, copies_a)
-    copies_b = exchange(1, send_mix.at[0], recv_mix.at[0])
-    gather_mixed(0, copies_b)
+    mix(0)
+    exchange(1, send_mix.at[0], recv_mix.at[0])
+    gather_mixed(0)
     for step in range(ROWS // 2):
         at = slice(step * 256, (step + 1) * 256)
         mid = jnp.concatenate([mid_row(0, 2 * step), mid_row(0, 2 * step + 1)], axis=1)
@@ -181,32 +184,35 @@
         values = (chan_pair[:, at] + update).astype(BF16).astype(F32)
         chan_pair[:, at] = values
         project(1, step, values)
-
-    copies_c = exchange(2, send_proj.at[1], recv_proj.at[1])
+        if step % 2 == 1:
+            send_half(step // 2, send_proj.at[1], recv_proj.at[1], 2)
+
+    recv_proj[1, me] = send_proj[1, me]
     half_gate_w = (gate_w[1].astype(F32) * 0.5).astype(BF16)
     for i in range(ROWS):
         at = slice(i * RES, (i + 1) * RES)
         row_gate[i] = 0.5 * jnp.tanh(contract(chan_normed[:, at], half_gate_w, 0, 0)) + 0.5
         row_pair[i] = chan_pair[:, at].T
-    mix(1, copies_c)
-    copies_d = exchange(3, send_mix.at[1], recv_mix.at[1])
-    gather_mixed(1, copies_d)
+    mix(1)
+    exchange(3, send_mix.at[1], recv_mix.at[1])
+    gather_mixed(1)
     for i in range(ROWS):
         update = row_gate[i] * contract(mid_row(1, i), out_w[1], 0, 0)
         result[i] = (row_pair[i] + update).astype(BF16)
 
-    for copies in (copies_a, copies_b, copies_c, copies_d):
-        for copy in copies:
-            copy.wait_send()
+    for block in range(2):
+        all_of(send_sem.at[2 * block], send_proj.at[block])
+        all_of(send_sem.at[2 * block + 1], send_mix.at[block])
 
 
 def per_device(pair_rep, proj_weight, gate_weight, out_weight, norm_gain, mid_gain):
-    vmem = pl.BlockSpec(memory_space=pltpu.VMEM)
+    operands = (pair_rep, proj_weight, gate_weight, out_weight, norm_gain, mid_gain)
+    operands = [pltpu.with_memory_space_constraint(value, pltpu.HBM) for value in operands]
     return pl.pallas_call(
         kernel,
         out_shape=jax.ShapeDtypeStruct((ROWS, RES, CHANS), BF16),
         in_specs=[pl.BlockSpec(memory_space=pltpu.HBM)] * 6,
-        out_specs=vmem,
+        out_specs=pl.BlockSpec(memory_space=pltpu.VMEM),
         scratch_shapes=[
             pltpu.VMEM((ROWS, RES, CHANS), BF16),
             pltpu.VMEM((2, CHANS, 4 * CHANS), BF16),
@@ -231,14 +237,14 @@
             pltpu.VMEM((RES * 2 * OWN, RES), F32),
             pltpu.VMEM((CHANS * ROWS, RES), F32),
             pltpu.VMEM((2, ROWS, RES), F32),
-            pltpu.SemaphoreType.DMA((4, len(OFFSETS))),
-            pltpu.SemaphoreType.DMA((4, len(OFFSETS))),
+            pltpu.SemaphoreType.DMA((4,)),
+            pltpu.SemaphoreType.DMA((4,)),
         ],
         compiler_params=pltpu.CompilerParams(
-            collective_id=0, has_side_effects=True, vmem_limit_bytes=63 * 1024 * 1024
+            collective_id=0, has_side_effects=True, vmem_limit_bytes=32 * 1024 * 1024
         ),
         name="triangles",
-    )(pair_rep, proj_weight, gate_weight, out_weight, norm_gain, mid_gain)
+    )(*operands)
 
 
 def solution(mesh):

time: 48.1 us -> 44.9 us (0.933)
  Pallas kernels: 46.2 us -> 44.1 us
  local copies, waits for them, and re-layouts: 1.67 us -> 0.71 us
    pallas_call x1, Pallas kernels: 46.2 us -> 44.1 us  [per_device(): pl.pallas_call(kernel, out_shape=jax.ShapeDtypeStruct((ROWS, RES, CHANS),...]
    unnamed x1, local copies, waits for them, and re-layouts: 1.67 us -> 0.71 us
where the time goes in v3:
time: 44.9 us; the launch traced here: 44.8 us
  Pallas kernels  44.1 us (98%)
  local copies, waits for them, and re-layouts  0.71 us (2%)
    pallas_call x1, Pallas kernels, per_device(): pl.pallas_call(kernel, out_shape=jax.ShapeDtypeStruct((ROWS, RES, CHANS),...  44.1 us

profile of v3, /device:TPU:2, one launch (start us, length us, event | category | flops | bytes accessed | tf_op | source)
XLA Modules:
  0.0 44.8 jit_solution(15968229516241179989)
XLA Ops:
  0.0 44.1 %triangles.1 = bf16[8,128,128]{2,1,0:T(8,128)(2,1)S(1)} custom-call(bf16[8,128,128]{2,1,0:T(8,128)(2,1)} %pair_hbm.1, bf16[2,128,512]{2,1,0:T(8,128)(2,1)} %proj_hbm.1, bf16[2,128,128]{2,1,0:T(8,128)(2,1)} %gate_hbm.1, bf16[2,128,128]{2,1,0:T(8,128)(2,1)} %out_hbm.1, f32[2,128]{1,0:T(2,128)} %norm_hbm.1, f32[2,128]{1,0:T(2,128)} %mid_hbm.1), custom_call_target="tpu_custom_call" | custom-call | tf_op jit(solution)/shard_map/triangles/pallas_call | solution.py:211
  44.1 0.7 %copy.8 = bf16[8,128,128]{2,1,0:T(8,128)(2,1)} copy(bf16[8,128,128]{2,1,0:T(8,128)(2,1)S(1)} %triangles.1) | data formatting | bytes 524288

commit v4 on v3

v4 whole, which is shorter than its diff:
```python
import jax
import jax.numpy as jnp
from jax import lax
from jax.experimental import pallas as pl
from jax.experimental.pallas import tpu as pltpu
from jax.sharding import PartitionSpec as P

MESH = pl.DeviceIdType.MESH
BF16 = jnp.bfloat16
F32 = jnp.float32
SIDE = 4
GROUP = SIDE * SIDE
RES = 128
CHANS = 128
ROWS = RES // GROUP
OWN = CHANS // GROUP
PART = OWN // 2
STEPS = ROWS // 2


def far_first(offset):
    return -sum(min(step, SIDE - step) for step in offset)


OFFSETS = sorted(
    [(dy, dx) for dy in range(SIDE) for dx in range(SIDE) if (dy, dx) != (0, 0)], key=far_first
)

PLAN = {1: ((0, 0, 2), (1, 0, 2)), 3: ((0, 2, 2), (1, 2, 2))}


def contract(lhs, rhs, lhs_dim, rhs_dim):
    return lax.dot_general(
        lhs, rhs, (((lhs_dim,), (rhs_dim,)), ((), ())), preferred_element_type=F32
    )


def kernel(
    pair_hbm, proj_hbm, gate_hbm, out_hbm, norm_hbm, mid_hbm, result,
    pair, proj_w, gate_w, out_w, norm_gain, mid_gain, load_sem, turned, proj_t, gate_t, out_t, gains, chan_pair, chan_normed, chan_gate, row_gate, row_pair,
    send_proj, recv_proj, send_mix, recv_mix, wide_proj, wide_mix, stats, send_sem, recv_sem,
):
    crop = lax.axis_index("dp")
    me = lax.axis_index("dap")
    y, x = me // SIDE, lax.rem(me, SIDE)

    def towards(offset):
        return lax.rem(y + offset[0], SIDE) * SIDE + lax.rem(x + offset[1], SIDE)

    places = (
        (proj_hbm, proj_w), (norm_hbm, norm_gain), (mid_hbm, mid_gain),
        (gate_hbm, gate_w), (out_hbm, out_w),
    )
    loads = [pltpu.make_async_copy(*place, load_sem.at[n]) for n, place in enumerate(places)]
    for step in range(STEPS):
        rows = pl.ds(2 * step, 2)
        loads.append(
            pltpu.make_async_copy(pair_hbm.at[rows], pair.at[rows], load_sem.at[5 + step])
        )
    for load in loads:
        load.start()

    barrier = pltpu.get_barrier_semaphore()
    for offset in OFFSETS:
        pl.semaphore_signal(
            barrier, inc=1, device_id=(crop, towards(offset)), device_id_type=MESH
        )

    def exchange(sem, source, target, cut=None):
        for offset in OFFSETS:
            there = towards(offset)
            from_ref, to_ref = source.at[there], target.at[me]
            if cut is not None:
                from_ref, to_ref = from_ref.at[pl.ds(*cut)], to_ref.at[pl.ds(*cut)]
            pltpu.make_async_remote_copy(
                src_ref=from_ref,
                dst_ref=to_ref,
                send_sem=send_sem.at[sem],
                recv_sem=recv_sem.at[sem],
                device_id=(crop, there),
                device_id_type=MESH,
            ).start()

    def exchange_projected(block, step):
        for part, *cut in PLAN.get(step, ()):
            exchange(4 * block + part, send_proj.at[block, part], recv_proj.at[block, part], cut)

    def all_of(sem, buffer):
        blocks = buffer.at[pl.ds(0, len(OFFSETS))]
        pltpu.make_async_copy(blocks, blocks, sem).wait()

    def column(row):
        return jnp.broadcast_to(row, (CHANS, CHANS)).T

    def turn_projection(block):
        for half in range(4):
            side, kind = half // 2, half % 2
            piece = proj_w[block, :, half * CHANS : (half + 1) * CHANS].astype(F32).T * 0.5
            for n in range(CHANS // PART):
                at = (2 * n + side) * PART
                turned[kind, at : at + PART, :] = piece[n * PART : (n + 1) * PART, :]
        for kind in range(2):
            proj_t[block, kind] = turned[kind].astype(BF16)

    def project(block, step, values):
        mean = jnp.mean(values, axis=0, keepdims=True)
        centered = values - mean
        var = jnp.mean(centered * centered, axis=0, keepdims=True)
        gain = gains[block]
        normed = centered * lax.rsqrt(var + 1e-05) * jnp.concatenate([gain, gain], axis=1)
        normed = normed.astype(BF16)
        chan_normed[:, step * 256 : (step + 1) * 256] = normed
        for half in range(2):
            at = slice(half * CHANS, (half + 1) * CHANS)
            half_value = contract(proj_t[block, 0, at], normed, 1, 0)
            half_gate = contract(proj_t[block, 1, at], normed, 1, 0)
            sides = half_value * jnp.tanh(half_gate) + half_value
            rows = [
                sides[:, h * RES : (h + 1) * RES].reshape(GROUP // 2, 2, 2 * PART, RES)
                for h in range(2)
            ]
            both = jnp.concatenate(rows, axis=2).astype(BF16)
            owners = slice(half * GROUP // 2, (half + 1) * GROUP // 2)
            for part in range(2):
                send_proj[block, part, owners, step] = both[:, part]

    def keep_own(sent, received):
        received[me] = sent[me]

    def mix(block):
        over = 1 if block == 0 else 0
        size = 2 * PART * ROWS
        for part in range(2):
            all_of(recv_sem.at[4 * block + part], recv_proj.at[block, part])
            for origin in range(GROUP):
                wide_proj[part, origin * size : (origin + 1) * size, :] = (
                    recv_proj[block, part, origin].astype(F32).reshape(size, RES)
                )
            for pair_of in range(PART // 2):
                mixed = []
                for c in (2 * pair_of, 2 * pair_of + 1):
                    left = wide_proj[part, pl.ds(c, RES, stride=2 * PART), :].astype(BF16)
                    right = wide_proj[part, pl.ds(PART + c, RES, stride=2 * PART), :].astype(BF16)
                    mixed.append(contract(left, right, over, over).reshape(GROUP, ROWS, RES))
                send_mix[block, part, :, pair_of] = jnp.concatenate(mixed, axis=1).astype(BF16)
            exchange(4 * block + 2 + part, send_mix.at[block, part], recv_mix.at[block, part])
            keep_own(send_mix.at[block, part], recv_mix.at[block, part])

    def gather_mixed(block):
        size = OWN * ROWS
        total = jnp.zeros((ROWS, RES), F32)
        for part in range(2):
            all_of(recv_sem.at[4 * block + 2 + part], recv_mix.at[block, part])
            for origin in range(GROUP):
                values = recv_mix[block, part, origin].astype(F32).reshape(PART * ROWS, RES)
                at = origin * size + part * PART * ROWS
                wide_mix[at : at + PART * ROWS, :] = values
                total = total + jnp.sum(values.reshape(PART, ROWS, RES), axis=0)
        mean = total * (1.0 / CHANS)
        spread = jnp.zeros_like(mean)
        for origin in range(GROUP):
            values = wide_mix[origin * size : (origin + 1) * size, :].reshape(OWN, ROWS, RES) - mean
            spread = spread + jnp.sum(values * values, axis=0)
        stats[0] = mean
        stats[1] = lax.rsqrt(spread * (1.0 / CHANS) + 1e-05)

    def mid_row(block, i):
        values = wide_mix[pl.ds(i, CHANS, stride=ROWS), :]
        mean, scale = stats[0, i : i + 1, :], stats[1, i : i + 1, :]
        return ((values - mean) * scale * gains[2 + block]).astype(BF16)

    loads[1].wait()
    loads[0].wait()
    gains[0] = column(norm_gain[0:1, :])
    turn_projection(0)
    for step in range(STEPS):
        loads[5 + step].wait()
        values = jnp.concatenate([pair[2 * step + h].astype(F32).T for h in range(2)], axis=1)
        chan_pair[:, step * 256 : (step + 1) * 256] = values
        project(0, step, values)
        if step == min(PLAN):
            pl.semaphore_wait(barrier, len(OFFSETS))
        exchange_projected(0, step)
    for part in range(2):
        keep_own(send_proj.at[0, part], recv_proj.at[0, part])

    for load in loads[2:5]:
        load.wait()
    gains[1] = column(norm_gain[1:2, :])
    gains[2] = column(mid_gain[0:1, :])
    gains[3] = column(mid_gain[1:2, :])
    turn_projection(1)
    gate_t[...] = (gate_w[0].astype(F32).T * 0.5).astype(BF16)
    out_t[...] = out_w[0].astype(F32).T.astype(BF16)
    for step in range(STEPS):
        at = slice(step * 256, (step + 1) * 256)
        chan_gate[:, at] = 0.5 * jnp.tanh(contract(gate_t[...], chan_normed[:, at], 1, 0)) + 0.5

    mix(0)
    gather_mixed(0)
    for step in range(STEPS):
        at = slice(step * 256, (step + 1) * 256)
        mid = jnp.concatenate([mid_row(0, 2 * step), mid_row(0, 2 * step + 1)], axis=1)
        update = chan_gate[:, at] * contract(out_t[...], mid, 1, 0)
        values = (chan_pair[:, at] + update).astype(BF16).astype(F32)
        chan_pair[:, at] = values
        project(1, step, values)
        exchange_projected(1, step)

    for part in range(2):
        keep_own(send_proj.at[1, part], recv_proj.at[1, part])
    half_gate_w = (gate_w[1].astype(F32) * 0.5).astype(BF16)
    for i in range(ROWS):
        at = slice(i * RES, (i + 1) * RES)
        row_gate[i] = 0.5 * jnp.tanh(contract(chan_normed[:, at], half_gate_w, 0, 0)) + 0.5
        row_pair[i] = chan_pair[:, at].T
    mix(1)
    gather_mixed(1)
    for i in range(ROWS):
        update = row_gate[i] * contract(mid_row(1, i), out_w[1], 0, 0)
        result[i] = (row_pair[i] + update).astype(BF16)

    for block in range(2):
        for part in range(2):
            all_of(send_sem.at[4 * block + part], send_proj.at[block, part])
            all_of(send_sem.at[4 * block + 2 + part], send_mix.at[block, part])


def per_device(pair_rep, proj_weight, gate_weight, out_weight, norm_gain, mid_gain):
    operands = (pair_rep, proj_weight, gate_weight, out_weight, norm_gain, mid_gain)
    operands = [pltpu.with_memory_space_constraint(value, pltpu.HBM) for value in operands]
    return pl.pallas_call(
        kernel,
        out_shape=jax.ShapeDtypeStruct((ROWS, RES, CHANS), BF16),
        in_specs=[pl.BlockSpec(memory_space=pltpu.HBM)] * 6,
        out_specs=pl.BlockSpec(memory_space=pltpu.VMEM),
        scratch_shapes=[
            pltpu.VMEM((ROWS, RES, CHANS), BF16),
            pltpu.VMEM((2, CHANS, 4 * CHANS), BF16),
            pltpu.VMEM((2, CHANS, CHANS), BF16),
            pltpu.VMEM((2, CHANS, CHANS), BF16),
            pltpu.VMEM((2, CHANS), F32),
            pltpu.VMEM((2, CHANS), F32),
            pltpu.SemaphoreType.DMA((5 + STEPS,)),
            pltpu.VMEM((2, 2 * CHANS, CHANS), F32),
            pltpu.VMEM((2, 2, 2 * CHANS, CHANS), BF16),
            pltpu.VMEM((CHANS, CHANS), BF16),
            pltpu.VMEM((CHANS, CHANS), BF16),
            pltpu.VMEM((4, CHANS, CHANS), F32),
            pltpu.VMEM((CHANS, ROWS * RES), F32),
            pltpu.VMEM((CHANS, ROWS * RES), BF16),
            pltpu.VMEM((CHANS, ROWS * RES), F32),
            pltpu.VMEM((ROWS, RES, CHANS), F32),
            pltpu.VMEM((ROWS, RES, CHANS), F32),
            pltpu.VMEM((2, 2, GROUP, STEPS, 4 * PART, RES), BF16),
            pltpu.VMEM((2, 2, GROUP, STEPS, 4 * PART, RES), BF16),
            pltpu.VMEM((2, 2, GROUP, PART // 2, 2 * ROWS, RES), BF16),
            pltpu.VMEM((2, 2, GROUP, PART // 2, 2 * ROWS, RES), BF16),
            pltpu.VMEM((2, RES * 2 * PART, RES), F32),
            pltpu.VMEM((CHANS * ROWS, RES), F32),
            pltpu.VMEM((2, ROWS, RES), F32),
            pltpu.SemaphoreType.DMA((8,)),
            pltpu.SemaphoreType.DMA((8,)),
        ],
        compiler_params=pltpu.CompilerParams(
            collective_id=0, has_side_effects=True, vmem_limit_bytes=32 * 1024 * 1024
        ),
        name="triangles",
    )(*operands)


def solution(mesh):
    return jax.shard_map(
        per_device,
        mesh=mesh,
        in_specs=(P(("dp", "dap"), None, None), P(), P(), P(), P(), P()),
        out_specs=P(("dp", "dap"), None, None),
        check_vma=False,
    )
```

time: 44.9 us -> 43.5 us (0.969)
  Pallas kernels: 44.1 us -> 42.7 us
    pallas_call x1, Pallas kernels: 44.1 us -> 42.7 us  [per_device(): pl.pallas_call(kernel, out_shape=jax.ShapeDtypeStruct((ROWS, RES, CHANS),...]
where the time goes in v4:
time: 43.5 us; the launch traced here: 43.4 us
  Pallas kernels  42.7 us (98%)
  local copies, waits for them, and re-layouts  0.71 us (2%)
    pallas_call x1, Pallas kernels, per_device(): pl.pallas_call(kernel, out_shape=jax.ShapeDtypeStruct((ROWS, RES, CHANS),...  42.7 us

profile of v4, /device:TPU:2, one launch (start us, length us, event | category | flops | bytes accessed | tf_op | source)
XLA Modules:
  0.0 43.4 jit_solution(14143763364615865883)
XLA Ops:
  0.0 42.7 %triangles.1 = bf16[8,128,128]{2,1,0:T(8,128)(2,1)S(1)} custom-call(bf16[8,128,128]{2,1,0:T(8,128)(2,1)} %pair_hbm.1, bf16[2,128,512]{2,1,0:T(8,128)(2,1)} %proj_hbm.1, bf16[2,128,128]{2,1,0:T(8,128)(2,1)} %gate_hbm.1, bf16[2,128,128]{2,1,0:T(8,128)(2,1)} %out_hbm.1, f32[2,128]{1,0:T(2,128)} %norm_hbm.1, f32[2,128]{1,0:T(2,128)} %mid_hbm.1), custom_call_target="tpu_custom_call" | custom-call | tf_op jit(solution)/shard_map/triangles/pallas_call | solution.py:232
  42.7 0.7 %copy.8 = bf16[8,128,128]{2,1,0:T(8,128)(2,1)} copy(bf16[8,128,128]{2,1,0:T(8,128)(2,1)S(1)} %triangles.1) | data formatting | bytes 524288

commit v5 on v4

--- a/solution.py
+++ b/solution.py
@@ -38,7 +38,7 @@
 def kernel(
     pair_hbm, proj_hbm, gate_hbm, out_hbm, norm_hbm, mid_hbm, result,
     pair, proj_w, gate_w, out_w, norm_gain, mid_gain, load_sem, turned, proj_t, gate_t, out_t, gains, chan_pair, chan_normed, chan_gate, row_gate, row_pair,
-    send_proj, recv_proj, send_mix, recv_mix, wide_proj, wide_mix, stats, send_sem, recv_sem,
+    send_proj, recv_proj, send_mix, recv_mix, wide_proj, wide_mix, stats, send_sem, recv_sem, entered,
 ):
     crop = lax.axis_index("dp")
     me = lax.axis_index("dap")
@@ -57,33 +57,58 @@
         loads.append(
             pltpu.make_async_copy(pair_hbm.at[rows], pair.at[rows], load_sem.at[5 + step])
         )
-    for load in loads:
+    for load in loads[:2] + loads[5:]:
         load.start()
 
     barrier = pltpu.get_barrier_semaphore()
-    for offset in OFFSETS:
-        pl.semaphore_signal(
-            barrier, inc=1, device_id=(crop, towards(offset)), device_id_type=MESH
-        )
+
+    @pl.when(me != 0)
+    def _():
+        for offset in OFFSETS:
+            pl.semaphore_signal(
+                barrier, inc=1, device_id=(crop, towards(offset)), device_id_type=MESH
+            )
+
+    @pl.when(me == 0)
+    def _():
+        pl.semaphore_wait(barrier, len(OFFSETS))
+        for offset in OFFSETS:
+            pl.semaphore_signal(
+                entered, inc=1, device_id=(crop, towards(offset)), device_id_type=MESH
+            )
+
+    for load in loads[2:5]:
+        load.start()
+
+    def send_to(there, sem, source, target, cut=None):
+        from_ref, to_ref = source.at[there], target.at[me]
+        if cut is not None:
+            from_ref, to_ref = from_ref.at[pl.ds(*cut)], to_ref.at[pl.ds(*cut)]
+        pltpu.make_async_remote_copy(
+            src_ref=from_ref,
+            dst_ref=to_ref,
+            send_sem=send_sem.at[sem],
+            recv_sem=recv_sem.at[sem],
+            device_id=(crop, there),
+            device_id_type=MESH,
+        ).start()
 
     def exchange(sem, source, target, cut=None):
         for offset in OFFSETS:
-            there = towards(offset)
-            from_ref, to_ref = source.at[there], target.at[me]
-            if cut is not None:
-                from_ref, to_ref = from_ref.at[pl.ds(*cut)], to_ref.at[pl.ds(*cut)]
-            pltpu.make_async_remote_copy(
-                src_ref=from_ref,
-                dst_ref=to_ref,
-                send_sem=send_sem.at[sem],
-                recv_sem=recv_sem.at[sem],
-                device_id=(crop, there),
-                device_id_type=MESH,
-            ).start()
-
-    def exchange_projected(block, step):
+            send_to(towards(offset), sem, source, target, cut)
+
+    def send_first(step):
         for part, *cut in PLAN.get(step, ()):
-            exchange(4 * block + part, send_proj.at[block, part], recv_proj.at[block, part], cut)
+            for offset in OFFSETS:
+                there = towards(offset)
+
+                @pl.when(there != 0)
+                def _():
+                    send_to(there, part, send_proj.at[0, part], recv_proj.at[0, part], cut)
+
+    def send_second(step):
+        for part, *cut in PLAN.get(step, ()):
+            exchange(4 + part, send_proj.at[1, part], recv_proj.at[1, part], cut)
 
     def all_of(sem, buffer):
         blocks = buffer.at[pl.ds(0, len(OFFSETS))]
@@ -179,8 +204,19 @@
         chan_pair[:, step * 256 : (step + 1) * 256] = values
         project(0, step, values)
         if step == min(PLAN):
-            pl.semaphore_wait(barrier, len(OFFSETS))
-        exchange_projected(0, step)
+
+            @pl.when(me != 0)
+            def _():
+                pl.semaphore_wait(barrier, len(OFFSETS) - 1)
+
+        send_first(step)
+
+    @pl.when(me != 0)
+    def _():
+        pl.semaphore_wait(entered, 1)
+        for part in range(2):
+            send_to(0, part, send_proj.at[0, part], recv_proj.at[0, part])
+
     for part in range(2):
         keep_own(send_proj.at[0, part], recv_proj.at[0, part])
 
@@ -205,7 +241,7 @@
         values = (chan_pair[:, at] + update).astype(BF16).astype(F32)
         chan_pair[:, at] = values
         project(1, step, values)
-        exchange_projected(1, step)
+        send_second(step)
 
     for part in range(2):
         keep_own(send_proj.at[1, part], recv_proj.at[1, part])
@@ -261,6 +297,7 @@
             pltpu.VMEM((2, ROWS, RES), F32),
             pltpu.SemaphoreType.DMA((8,)),
             pltpu.SemaphoreType.DMA((8,)),
+            pltpu.SemaphoreType.REGULAR,
         ],
         compiler_params=pltpu.CompilerParams(
             collective_id=0, has_side_effects=True, vmem_limit_bytes=32 * 1024 * 1024

time: 43.5 us -> 40.2 us (0.924)
  Pallas kernels: 42.7 us -> 39.3 us
    pallas_call x1, Pallas kernels: 42.7 us -> 39.3 us  [per_device(): pl.pallas_call(kernel, out_shape=jax.ShapeDtypeStruct((ROWS, RES, CHANS),...]
where the time goes in v5:
time: 40.2 us; the launch traced here: 40 us
  Pallas kernels  39.3 us (98%)
  local copies, waits for them, and re-layouts  0.71 us (2%)
    pallas_call x1, Pallas kernels, per_device(): pl.pallas_call(kernel, out_shape=jax.ShapeDtypeStruct((ROWS, RES, CHANS),...  39.3 us

profile of v5, /device:TPU:2, one launch (start us, length us, event | category | flops | bytes accessed | tf_op | source)
XLA Modules:
  0.0 40.0 jit_solution(10878281130939059992)
XLA Ops:
  0.0 39.3 %triangles.1 = bf16[8,128,128]{2,1,0:T(8,128)(2,1)S(1)} custom-call(bf16[8,128,128]{2,1,0:T(8,128)(2,1)} %pair_hbm.1, bf16[2,128,512]{2,1,0:T(8,128)(2,1)} %proj_hbm.1, bf16[2,128,128]{2,1,0:T(8,128)(2,1)} %gate_hbm.1, bf16[2,128,128]{2,1,0:T(8,128)(2,1)} %out_hbm.1, f32[2,128]{1,0:T(2,128)} %norm_hbm.1, f32[2,128]{1,0:T(2,128)} %mid_hbm.1), custom_call_target="tpu_custom_call" | custom-call | tf_op jit(solution)/shard_map/triangles/pallas_call | solution.py:268
  39.3 0.7 %copy.8 = bf16[8,128,128]{2,1,0:T(8,128)(2,1)} copy(bf16[8,128,128]{2,1,0:T(8,128)(2,1)S(1)} %triangles.1) | data formatting | bytes 524288

commit v6 on v5

--- a/solution.py
+++ b/solution.py
@@ -26,7 +26,10 @@
     [(dy, dx) for dy in range(SIDE) for dx in range(SIDE) if (dy, dx) != (0, 0)], key=far_first
 )
 
-PLAN = {1: ((0, 0, 2), (1, 0, 2)), 3: ((0, 2, 2), (1, 2, 2))}
+PLAN = (
+    {1: ((0, 0, 2), (1, 0, 2)), 3: ((0, 2, 2), (1, 2, 2))},
+    {1: ((0, 0, 2),), 3: ((0, 2, 2), (1, 0, 4))},
+)
 
 
 def contract(lhs, rhs, lhs_dim, rhs_dim):
@@ -37,7 +40,7 @@
 
 def kernel(
     pair_hbm, proj_hbm, gate_hbm, out_hbm, norm_hbm, mid_hbm, result,
-    pair, proj_w, gate_w, out_w, norm_gain, mid_gain, load_sem, turned, proj_t, gate_t, out_t, gains, chan_pair, chan_normed, chan_gate, row_gate, row_pair,
+    pair, proj_w, gate_w, out_w, norm_gain, mid_gain, load_sem, picks, proj_t, gate_t, out_t, gains, chan_pair, chan_normed, chan_gate, row_gate, row_pair,
     send_proj, recv_proj, send_mix, recv_mix, wide_proj, wide_mix, stats, send_sem, recv_sem, entered,
 ):
     crop = lax.axis_index("dp")
@@ -57,9 +60,6 @@
         loads.append(
             pltpu.make_async_copy(pair_hbm.at[rows], pair.at[rows], load_sem.at[5 + step])
         )
-    for load in loads[:2] + loads[5:]:
-        load.start()
-
     barrier = pltpu.get_barrier_semaphore()
 
     @pl.when(me != 0)
@@ -77,8 +77,10 @@
                 entered, inc=1, device_id=(crop, towards(offset)), device_id_type=MESH
             )
 
-    for load in loads[2:5]:
+    for load in loads:
         load.start()
+
+    members = [towards(offset) for offset in OFFSETS]
 
     def send_to(there, sem, source, target, cut=None):
         from_ref, to_ref = source.at[there], target.at[me]
@@ -94,20 +96,19 @@
         ).start()
 
     def exchange(sem, source, target, cut=None):
-        for offset in OFFSETS:
-            send_to(towards(offset), sem, source, target, cut)
+        for there in members:
+            send_to(there, sem, source, target, cut)
 
     def send_first(step):
-        for part, *cut in PLAN.get(step, ()):
-            for offset in OFFSETS:
-                there = towards(offset)
+        for part, *cut in PLAN[0].get(step, ()):
+            for there in members:
 
                 @pl.when(there != 0)
                 def _():
                     send_to(there, part, send_proj.at[0, part], recv_proj.at[0, part], cut)
 
     def send_second(step):
-        for part, *cut in PLAN.get(step, ()):
+        for part, *cut in PLAN[1].get(step, ()):
             exchange(4 + part, send_proj.at[1, part], recv_proj.at[1, part], cut)
 
     def all_of(sem, buffer):
@@ -117,24 +118,35 @@
     def column(row):
         return jnp.broadcast_to(row, (CHANS, CHANS)).T
 
+    def pick(side):
+        row = lax.broadcasted_iota(jnp.int32, (2 * CHANS, CHANS), 0)
+        column_of = lax.broadcasted_iota(jnp.int32, (2 * CHANS, CHANS), 1)
+        group, place = row // PART, lax.rem(row, PART)
+        hit = (lax.rem(group, 2) == side) & (column_of == (group // 2) * PART + place)
+        return jnp.where(hit, 0.5, 0.0).astype(BF16)
+
+    for side in range(2):
+        picks[side] = pick(side)
+
     def turn_projection(block):
-        for half in range(4):
-            side, kind = half // 2, half % 2
-            piece = proj_w[block, :, half * CHANS : (half + 1) * CHANS].astype(F32).T * 0.5
-            for n in range(CHANS // PART):
-                at = (2 * n + side) * PART
-                turned[kind, at : at + PART, :] = piece[n * PART : (n + 1) * PART, :]
         for kind in range(2):
-            proj_t[block, kind] = turned[kind].astype(BF16)
-
-    def project(block, step, values):
+            turned = jnp.zeros((2 * CHANS, CHANS), F32)
+            for side in range(2):
+                at = (2 * side + kind) * CHANS
+                piece = proj_w[block, :, at : at + CHANS]
+                turned = turned + contract(picks[side], piece, 1, 1)
+            proj_t[block, kind] = turned.astype(BF16)
+
+    def normalize(block, step, values):
         mean = jnp.mean(values, axis=0, keepdims=True)
         centered = values - mean
         var = jnp.mean(centered * centered, axis=0, keepdims=True)
         gain = gains[block]
         normed = centered * lax.rsqrt(var + 1e-05) * jnp.concatenate([gain, gain], axis=1)
-        normed = normed.astype(BF16)
-        chan_normed[:, step * 256 : (step + 1) * 256] = normed
+        chan_normed[:, step * 256 : (step + 1) * 256] = normed.astype(BF16)
+
+    def project(block, step):
+        normed = chan_normed[:, step * 256 : (step + 1) * 256]
         for half in range(2):
             at = slice(half * CHANS, (half + 1) * CHANS)
             half_value = contract(proj_t[block, 0, at], normed, 1, 0)
@@ -198,18 +210,20 @@
     loads[0].wait()
     gains[0] = column(norm_gain[0:1, :])
     turn_projection(0)
-    for step in range(STEPS):
-        loads[5 + step].wait()
-        values = jnp.concatenate([pair[2 * step + h].astype(F32).T for h in range(2)], axis=1)
-        chan_pair[:, step * 256 : (step + 1) * 256] = values
-        project(0, step, values)
-        if step == min(PLAN):
-
-            @pl.when(me != 0)
-            def _():
-                pl.semaphore_wait(barrier, len(OFFSETS) - 1)
-
-        send_first(step)
+    @pl.when(me != 0)
+    def _():
+        pl.semaphore_wait(barrier, len(OFFSETS) - 1)
+
+    for first in range(0, STEPS, 2):
+        steps = range(first, first + 2)
+        for step in steps:
+            loads[5 + step].wait()
+            values = jnp.concatenate([pair[2 * step + h].astype(F32).T for h in range(2)], axis=1)
+            chan_pair[:, step * 256 : (step + 1) * 256] = values
+            normalize(0, step, values)
+        for step in steps:
+            project(0, step)
+            send_first(step)
 
     @pl.when(me != 0)
     def _():
@@ -234,14 +248,18 @@
 
     mix(0)
     gather_mixed(0)
-    for step in range(STEPS):
-        at = slice(step * 256, (step + 1) * 256)
-        mid = jnp.concatenate([mid_row(0, 2 * step), mid_row(0, 2 * step + 1)], axis=1)
-        update = chan_gate[:, at] * contract(out_t[...], mid, 1, 0)
-        values = (chan_pair[:, at] + update).astype(BF16).astype(F32)
-        chan_pair[:, at] = values
-        project(1, step, values)
-        send_second(step)
+    for first in range(0, STEPS, 2):
+        steps = range(first, first + 2)
+        for step in steps:
+            at = slice(step * 256, (step + 1) * 256)
+            mid = jnp.concatenate([mid_row(0, 2 * step), mid_row(0, 2 * step + 1)], axis=1)
+            update = chan_gate[:, at] * contract(out_t[...], mid, 1, 0)
+            values = (chan_pair[:, at] + update).astype(BF16).astype(F32)
+            chan_pair[:, at] = values
+            normalize(1, step, values)
+        for step in steps:
+            project(1, step)
+            send_second(step)
 
     for part in range(2):
         keep_own(send_proj.at[1, part], recv_proj.at[1, part])
@@ -278,7 +296,7 @@
             pltpu.VMEM((2, CHANS), F32),
             pltpu.VMEM((2, CHANS), F32),
             pltpu.SemaphoreType.DMA((5 + STEPS,)),
-            pltpu.VMEM((2, 2 * CHANS, CHANS), F32),
+            pltpu.VMEM((2, 2 * CHANS, CHANS), BF16),
             pltpu.VMEM((2, 2, 2 * CHANS, CHANS), BF16),
             pltpu.VMEM((CHANS, CHANS), BF16),
             pltpu.VMEM((CHANS, CHANS), BF16),

time: 40.2 us -> 40 us (level)
  no operation moved by 1% of the time
where the time goes in v6:
time: 40 us; the launch traced here: 39.9 us
  Pallas kernels  39.1 us (98%)
  local copies, waits for them, and re-layouts  0.71 us (2%)
    pallas_call x1, Pallas kernels, per_device(): pl.pallas_call(kernel, out_shape=jax.ShapeDtypeStruct((ROWS, RES, CHANS),...  39.1 us

profile of v6, /device:TPU:2, one launch (start us, length us, event | category | flops | bytes accessed | tf_op | source)
XLA Modules:
  0.0 39.9 jit_solution(5962106024756183637)
XLA Ops:
  0.0 39.1 %triangles.1 = bf16[8,128,128]{2,1,0:T(8,128)(2,1)S(1)} custom-call(bf16[8,128,128]{2,1,0:T(8,128)(2,1)} %pair_hbm.1, bf16[2,128,512]{2,1,0:T(8,128)(2,1)} %proj_hbm.1, bf16[2,128,128]{2,1,0:T(8,128)(2,1)} %gate_hbm.1, bf16[2,128,128]{2,1,0:T(8,128)(2,1)} %out_hbm.1, f32[2,128]{1,0:T(2,128)} %norm_hbm.1, f32[2,128]{1,0:T(2,128)} %mid_hbm.1), custom_call_target="tpu_custom_call" | custom-call | tf_op jit(solution)/shard_map/triangles/pallas_call | solution.py:286
  39.2 0.7 %copy.8 = bf16[8,128,128]{2,1,0:T(8,128)(2,1)} copy(bf16[8,128,128]{2,1,0:T(8,128)(2,1)S(1)} %triangles.1) | data formatting | bytes 524288

commit v7 on v6

--- a/solution.py
+++ b/solution.py
@@ -27,7 +27,7 @@
 )
 
 PLAN = (
-    {1: ((0, 0, 2), (1, 0, 2)), 3: ((0, 2, 2), (1, 2, 2))},
+    {1: ((0, 0, 2),), 3: ((0, 2, 2), (1, 0, 4))},
     {1: ((0, 0, 2),), 3: ((0, 2, 2), (1, 0, 4))},
 )
 

time: 40 us -> 39.8 us (level)
  no operation moved by 1% of the time
where the time goes in v7:
time: 39.8 us; the launch traced here: 39.6 us
  Pallas kernels  38.9 us (98%)
  local copies, waits for them, and re-layouts  0.71 us (2%)
    pallas_call x1, Pallas kernels, per_device(): pl.pallas_call(kernel, out_shape=jax.ShapeDtypeStruct((ROWS, RES, CHANS),...  38.9 us

profile of v7, /device:TPU:2, one launch (start us, length us, event | category | flops | bytes accessed | tf_op | source)
XLA Modules:
  0.0 39.6 jit_solution(6738150356548589162)
XLA Ops:
  0.0 38.9 %triangles.1 = bf16[8,128,128]{2,1,0:T(8,128)(2,1)S(1)} custom-call(bf16[8,128,128]{2,1,0:T(8,128)(2,1)} %pair_hbm.1, bf16[2,128,512]{2,1,0:T(8,128)(2,1)} %proj_hbm.1, bf16[2,128,128]{2,1,0:T(8,128)(2,1)} %gate_hbm.1, bf16[2,128,128]{2,1,0:T(8,128)(2,1)} %out_hbm.1, f32[2,128]{1,0:T(2,128)} %norm_hbm.1, f32[2,128]{1,0:T(2,128)} %mid_hbm.1), custom_call_target="tpu_custom_call" | custom-call | tf_op jit(solution)/shard_map/triangles/pallas_call | solution.py:286
  38.9 0.7 %copy.8 = bf16[8,128,128]{2,1,0:T(8,128)(2,1)} copy(bf16[8,128,128]{2,1,0:T(8,128)(2,1)S(1)} %triangles.1) | data formatting | bytes 524288

commit v8 on v7

--- a/solution.py
+++ b/solution.py
@@ -60,6 +60,9 @@
         loads.append(
             pltpu.make_async_copy(pair_hbm.at[rows], pair.at[rows], load_sem.at[5 + step])
         )
+    for load in loads[:2] + loads[5:]:
+        load.start()
+
     barrier = pltpu.get_barrier_semaphore()
 
     @pl.when(me != 0)
@@ -77,7 +80,7 @@
                 entered, inc=1, device_id=(crop, towards(offset)), device_id_type=MESH
             )
 
-    for load in loads:
+    for load in loads[2:5]:
         load.start()
 
     members = [towards(offset) for offset in OFFSETS]

time: 39.8 us -> 39.8 us (level)
  no operation moved by 1% of the time
where the time goes in v8:
time: 39.8 us; the launch traced here: 39.6 us
  Pallas kernels  38.9 us (98%)
  local copies, waits for them, and re-layouts  0.71 us (2%)
    pallas_call x1, Pallas kernels, per_device(): pl.pallas_call(kernel, out_shape=jax.ShapeDtypeStruct((ROWS, RES, CHANS),...  38.9 us

profile of v8, /device:TPU:2, one launch (start us, length us, event | category | flops | bytes accessed | tf_op | source)
XLA Modules:
  0.0 39.6 jit_solution(10669748460325546429)
XLA Ops:
  0.0 38.9 %triangles.1 = bf16[8,128,128]{2,1,0:T(8,128)(2,1)S(1)} custom-call(bf16[8,128,128]{2,1,0:T(8,128)(2,1)} %pair_hbm.1, bf16[2,128,512]{2,1,0:T(8,128)(2,1)} %proj_hbm.1, bf16[2,128,128]{2,1,0:T(8,128)(2,1)} %gate_hbm.1, bf16[2,128,128]{2,1,0:T(8,128)(2,1)} %out_hbm.1, f32[2,128]{1,0:T(2,128)} %norm_hbm.1, f32[2,128]{1,0:T(2,128)} %mid_hbm.1), custom_call_target="tpu_custom_call" | custom-call | tf_op jit(solution)/shard_map/triangles/pallas_call | solution.py:289
  38.9 0.7 %copy.8 = bf16[8,128,128]{2,1,0:T(8,128)(2,1)} copy(bf16[8,128,128]{2,1,0:T(8,128)(2,1)S(1)} %triangles.1) | data formatting | bytes 524288
